TPU v7x, 32 devices: a whole 2x2x4 slice. The times are simulated.
32 devices in a mesh: dp: 8 (over y, x, core), expert: 4 (over z).
Axes of the slice: x: 2, y: 2, z: 4, core: 2. Of those that a mesh axis runs over, the one named last changes fastest.
Arguments:
- grad: bfloat16 [4, 8, 256, 8192], P('expert', 'dp'), may hold values from -23 to 23, as said below
- error: bfloat16 [4, 8, 256, 8192], P('expert', 'dp'), may hold values from -3 to 3
- q_init: bfloat16 [4, 32, 8192], P('expert'), may hold values from -4 to 4
Outputs:
- basis_out: float32 [4, 256, 32], P('expert')
- q_factor: float32 [4, 32, 8192], P('expert', None, 'dp')
- new_error: bfloat16 [4, 8, 256, 8192], P('expert', 'dp')
- error_norm: float32 [], replicated
Inputs may be any that keep to these rules, and one draw needn't show every extreme that they name: `grad`: entries of each expert's gradient.
All inputs are finite; a program needn't handle non-finite values.
Results may differ from a plain program's by a relative error of at most 0.02.
Values may be sent and summed in bfloat16 or wider, within the bound.
A program may use at most 64 MiB of HBM per device.

v0:
```python
import jax
import jax.numpy as jnp
from jax import lax
from jax.sharding import PartitionSpec as P

ITERS = 2


def make_orthonormal(lower_factor, projected):
    solved = jax.scipy.linalg.solve_triangular(
        lower_factor, jnp.swapaxes(projected, 1, 2), lower=True
    )
    return jnp.swapaxes(solved, 1, 2)


def gram_of(projected):
    return jnp.einsum("erk,erj->ekj", projected, projected, precision=lax.Precision.HIGHEST)


def local(grad, error, q_init):
    combined = (grad[:, 0].astype(jnp.float32) + error[:, 0].astype(jnp.float32)).astype(
        jnp.bfloat16
    )
    replicas = lax.axis_size("dp")
    groups = lax.axis_size("expert")
    share_width = combined.shape[2] // replicas
    factor_low = q_init
    orthonormal = jnp.zeros((combined.shape[0], combined.shape[1], q_init.shape[1]), jnp.float32)
    ortho_low = orthonormal.astype(jnp.bfloat16)
    factor_share = jnp.zeros((q_init.shape[0], q_init.shape[1], share_width), jnp.float32)
    for step in range(ITERS):
        partial_value = jnp.einsum(
            "erf,ekf->erk", combined, factor_low, preferred_element_type=jnp.float32
        )
        projected = lax.psum(partial_value, "dp") / replicas
        lower_factor = jnp.linalg.cholesky(gram_of(projected))
        orthonormal = make_orthonormal(lower_factor, projected)
        ortho_low = orthonormal.astype(jnp.bfloat16)
        right_part = jnp.einsum(
            "erk,erf->ekf", ortho_low, combined, preferred_element_type=jnp.float32
        )
        factor_full = lax.psum(right_part.astype(jnp.bfloat16), "dp").astype(jnp.float32) / replicas
        factor_low = factor_full.astype(jnp.bfloat16)
        factor_share = lax.dynamic_slice_in_dim(
            factor_full, lax.axis_index("dp") * share_width, share_width, 2
        )
    approx = jnp.einsum("erk,ekf->erf", ortho_low, factor_low, preferred_element_type=jnp.float32)
    new_error = (combined.astype(jnp.float32) - approx).astype(jnp.bfloat16)
    local_sum = jnp.sum(jnp.square(new_error.astype(jnp.float32)))
    total = lax.psum(local_sum, ("dp", "expert"))
    count = combined.shape[0] * combined.shape[1] * combined.shape[2] * replicas * groups
    error_norm = jnp.sqrt(total / count)
    return (orthonormal, factor_share, new_error[:, None], error_norm)


def solution(mesh):
    placed = (P("expert", "dp", None, None), P("expert", "dp", None, None), P("expert", None, None))
    return jax.shard_map(
        local,
        mesh=mesh,
        in_specs=placed,
        out_specs=(
            P("expert", None, None),
            P("expert", None, "dp"),
            P("expert", "dp", None, None),
            P(),
        ),
        check_vma=False,
    )
```

profile of v0, /device:TPU:0, one launch (start us, length us, event | category | flops | bytes accessed | tf_op | source)
XLA Modules:
  0.0 252.6 jit_solution(3538474910117702679)
XLA Ops:
  7.2 0.0 copy-start
  7.2 0.0 all-reduce.3.cloned.1.call-start
  7.2 5.1 %fusion.3 = bf16[256,8192]{1,0:T(8,128)(2,1)S(1)} fusion(bf16[1,1,256,8192]{3,2,1,0:T(8,128)(2,1)} %param.7, bf16[1,1,256,8192]{3,2,1,0:T(8,128)(2,1)} %param.6), kind=kLoop, calls=%fused_computation.8 | loop fusion | flops 8388608 | bytes 12582912 | tf_op jit(solution)/shard_map/convert_element_type | solution.py:21
  12.3 0.0 copy-start.1
  12.3 2.0 copy-done.1
  14.3 0.0 copy-done
  14.3 1.4 convolution_bitcast_fusion.3
  15.7 25.5 %psum.35 = f32[1,256,32]{1,2,0:T(8,128)S(1)} all-reduce(f32[1,256,32]{1,2,0:T(8,128)S(1)} %convolution_bitcast_fusion.3), channel_id=1, replica_groups=mesh['dp'=8,'expert'=4] {'dp'}, use_global_device_ids=true, to_apply=%region_0.0 | all-reduce | flops 8192 | bytes 65536 | tf_op jit(solution)/shard_map/psum | solution.py:35
  41.2 0.2 fusion.16
  41.4 0.1 copy.8
  41.4 2.9 %custom-call.8 = f32[1,32,32]{2,1,0:T(8,128)S(1)} custom-call(f32[1,32,32]{2,1,0:T(8,128)S(1)} %fusion.23), custom_call_target="Cholesky" | custom-call | tf_op jit(solution)/shard_map/jit(cholesky)/cholesky | solution.py:36
  44.4 0.6 compare_reduce_fusion.1
  45.0 0.7 select_select_fusion.1
  45.7 2.4 custom-call.9
  48.1 0.2 fusion.5
  48.4 3.8 %fusion.1 = bf16[1,32,8192]{2,1,0:T(8,128)(2,1)} fusion(bf16[256,32]{0,1:T(8,128)(2,1)S(1)} %fusion.5, bf16[256,8192]{1,0:T(8,128)(2,1)} %copy-done.1), kind=kOutput, calls=%fused_computation.4 | convolution fusion | flops 134479872 | bytes 4734976 | tf_op jit(solution)/shard_map/erk,erf->ekf/dot_general | solution.py:39
  52.2 0.0 all-reduce.3.cloned.1.call-update
  52.3 0.0 all-reduce.5.cloned.1.call-start
  52.3 54.0 %all-reduce.3.cloned.1.call-done = bf16[1,32,8192]{2,1,0:T(8,128)(2,1)} async-done(((bf16[1,32,8192]{2,1,0:T(8,128)(2,1)}), bf16[1,32,8192]{2,1,0:T(8,128)(2,1)}) %all-reduce.3.cloned.1.call-update) | async-done | bytes 524304 | tf_op jit(solution)/shard_map/psum | solution.py:42
  106.3 3.7 %convolution_bitcast_fusion.1 = f32[1,256,32]{1,2,0:T(8,128)S(1)} fusion(bf16[256,8192]{1,0:T(8,128)(2,1)} %copy-done.1, bf16[1,32,8192]{2,1,0:T(8,128)(2,1)} %all-reduce.3.cloned.1.call-done), kind=kOutput, calls=%fused_computation.10 | convolution fusion | flops 135004160 | bytes 4751360 | tf_op jit(solution)/shard_map/erf,ekf->erk/dot_general | solution.py:32
  110.0 22.4 %psum.37 = f32[1,256,32]{1,2,0:T(8,128)S(1)} all-reduce(f32[1,256,32]{1,2,0:T(8,128)S(1)} %convolution_bitcast_fusion.1), channel_id=1, replica_groups=mesh['dp'=8,'expert'=4] {'dp'}, use_global_device_ids=true, to_apply=%region_4.0 | all-reduce | flops 8192 | bytes 65536 | tf_op jit(solution)/shard_map/psum | solution.py:35
  132.3 0.2 fusion.14
  132.5 0.1 copy.10
  132.6 2.9 %custom-call.10 = f32[1,32,32]{2,1,0:T(8,128)S(1)} custom-call(f32[1,32,32]{2,1,0:T(8,128)S(1)} %fusion.22), custom_call_target="Cholesky" | custom-call | tf_op jit(solution)/shard_map/jit(cholesky)/cholesky | solution.py:36
  135.6 0.6 compare_reduce_fusion
  136.2 0.7 select_select_fusion
  136.9 2.4 custom-call.11
  139.3 0.2 convolution_bitcast_fusion
  139.5 0.0 copy-start.3
  139.6 3.8 %fusion.2 = bf16[1,32,8192]{2,1,0:T(8,128)(2,1)} fusion(bf16[256,8192]{1,0:T(8,128)(2,1)} %copy-done.1, f32[1,256,32]{1,2,0:T(8,128)S(1)} %convolution_bitcast_fusion), kind=kOutput, calls=%fused_computation.5 | convolution fusion | flops 134488064 | bytes 4751360 | tf_op jit(solution)/shard_map/erk,erf->ekf/dot_general | solution.py:39
  143.4 0.0 all-reduce.5.cloned.1.call-update
  143.4 54.0 %all-reduce.5.cloned.1.call-done = bf16[1,32,8192]{2,1,0:T(8,128)(2,1)} async-done(((bf16[1,32,8192]{2,1,0:T(8,128)(2,1)}), bf16[1,32,8192]{2,1,0:T(8,128)(2,1)}) %all-reduce.5.cloned.1.call-update) | async-done | bytes 524304 | tf_op jit(solution)/shard_map/psum | solution.py:42
  197.4 0.0 copy-start.2
  197.4 6.4 %multiply_reduce_fusion = (f32[]{:T(128)}, bf16[256,8192]{1,0:T(8,128)(2,1)}) fusion(bf16[1,32,8192]{2,1,0:T(8,128)(2,1)} %all-reduce.5.cloned.1.call-done, f32[1,256,32]{1,2,0:T(8,128)S(1)} %convolution_bitcast_fusion, bf16[256,8192]{1,0:T(8,128)(2,1)} %copy-done.1), kind=kOutput, calls=%fused_computation.6 | convolution fusion | flops 147595264 | bytes 8945668 | tf_op jit(solution)/shard_map/erk,ekf->erf/dot_general | solution.py:47
  203.8 0.0 copy-done.3
  203.8 39.5 %psum.39 = f32[]{:T(128)} all-reduce(f32[]{:T(128)} %get-tuple-element.6), channel_id=1, replica_groups=mesh['dp'=8,'expert'=4] {'dp','expert'}, use_global_device_ids=true, to_apply=%region_7.10 | all-reduce | flops 1 | bytes 8 | tf_op jit(solution)/shard_map/psum | solution.py:50
  243.9 0.0 copy-done.2
  243.9 0.1 convert_multiply_fusion
  244.0 0.7 constant_dynamic-slice_fusion
  (4 shorter events, 0.1 us)
Async XLA Ops:
  7.2 7.1 %copy-start = (bf16[1,32,8192]{2,1,0:T(8,128)(2,1)S(1)}, bf16[1,32,8192]{2,1,0:T(8,128)(2,1)}, u32[]{:S(2)}) copy-start(bf16[1,32,8192]{2,1,0:T(8,128)(2,1)} %param.8) | copy-start | bytes 1572868
  7.2 99.1 %all-reduce.3.cloned.1.call-start = ((), (), s32[]{:S(2)}) async-start(), calls=%async_computation | async-start | bytes 1048576 | tf_op jit(solution)/shard_map/psum | solution.py:42
  12.3 2.0 copy-start.1
  52.3 145.1 %all-reduce.5.cloned.1.call-start = ((), (), s32[]{:S(2)}) async-start(), calls=%async_computation.1 | async-start | bytes 1048576 | tf_op jit(solution)/shard_map/psum | solution.py:42
  139.5 64.2 %copy-start.3 = (f32[1,256,32]{1,2,0:T(8,128)}, f32[1,256,32]{1,2,0:T(8,128)S(1)}, u32[]{:S(2)}) copy-start(f32[1,256,32]{1,2,0:T(8,128)S(1)} %convolution_bitcast_fusion) | copy-start | bytes 98308
  197.4 46.5 %copy-start.2 = (bf16[1,32,8192]{2,1,0:T(8,128)(2,1)S(1)}, bf16[1,32,8192]{2,1,0:T(8,128)(2,1)}, u32[]{:S(2)}) copy-start(bf16[1,32,8192]{2,1,0:T(8,128)(2,1)} %all-reduce.5.cloned.1.call-done) | copy-start | bytes 1572868
Sparse Core Ops, SparseCore 0:
  52.4 53.8 all-reduce.2
  143.5 53.7 all-reduce.4
where the time goes:
time: 253 us
  waiting for transfers between devices  108 us (43%)
  blocking collectives  87.3 us (35%)
  matrix products  19.9 us (8%)
  other arithmetic  18.5 us (7%)
  between operations  16 us (6%)
  local copies, waits for them, and re-layouts  2.84 us (1%)
    psum x2, waiting for transfers between devices, local(): lax.psum(right_part.astype(jnp.bfloat16), 'dp').astype(jnp.float32)  108 us
    psum x2, blocking collectives, local(): projected = lax.psum(partial_value, 'dp') / replicas  47.9 us
    psum x1, blocking collectives, local(): total = lax.psum(local_sum, ('dp', 'expert'))  39.5 us
    dot_general x2, matrix products, local(): jnp.einsum('erk,erf->ekf', ortho_low, combined, preferred_element_type=jn...  7.68 us
    another operation x6, other arithmetic, local(): lower_factor = jnp.linalg.cholesky(gram_of(projected))  7.19 us
    dot_general x1, matrix products, local(): jnp.einsum('erk,ekf->erf', ortho_low, factor_low, preferred_element_type=...  6.38 us
    another operation x4, other arithmetic, make_orthonormal(): jax.scipy.linalg.solve_triangular(lower_factor, jnp.swapaxes(projected, 1...  6.17 us
  transfers between devices with their start and end apart: 2, of which 2 were waited for; matrix products, arithmetic and copies ran while one was open for 0% of the time, Pallas kernels for 0%

commit v1 on v0

v1 whole, which is shorter than its diff:
```python
import functools

import jax
import jax.numpy as jnp
from jax import lax
from jax.experimental import pallas as pl
from jax.experimental.pallas import tpu as pltpu
from jax.sharding import PartitionSpec as P

ITERS = 2
MESH = pl.DeviceIdType.MESH
F32 = jnp.float32
BF16 = jnp.bfloat16
LANES = 128
GROUP = 8
NT = (((1,), (1,)), ((), ()))


def xor(a, b, size):
    out, bit = 0, 1
    while bit < size:
        out = out + bit * lax.rem(lax.div(a, bit) + lax.div(b, bit), 2)
        bit *= 2
    return out


def spread_row(tile, j):
    return jnp.broadcast_to(tile[j : j + 1, :], tile.shape)


def orthonormal_rows(pt):
    rank, rows = pt.shape
    groups, halves = rank // GROUP, rows // LANES
    padded = jnp.concatenate([pt, jnp.zeros((LANES - rank, rows), F32)], axis=0)
    gram = lax.dot_general(pt, padded, NT, precision=lax.Precision.HIGHEST, preferred_element_type=F32)
    g = [gram[GROUP * i : GROUP * (i + 1), :] for i in range(groups)]
    x = [
        [pt[GROUP * i : GROUP * (i + 1), LANES * h : LANES * (h + 1)] for h in range(halves)]
        for i in range(groups)
    ]
    row_id = lax.broadcasted_iota(jnp.int32, (GROUP, LANES), 0)
    for b in range(groups):
        below = range(b, groups)
        col = [
            {i: jnp.broadcast_to(g[i][:, GROUP * b + j : GROUP * b + j + 1], (GROUP, LANES)) for i in below}
            for j in range(GROUP)
        ]
        pivots = jnp.ones((GROUP, LANES), F32)
        for j in range(GROUP):
            pivot = spread_row(col[j][b], j)
            pivots = jnp.where(row_id == j, pivot, pivots)
            inverse = 1.0 / pivot
            factor = {i: col[j][i] * inverse for i in below}
            factor[b] = jnp.where(row_id > j, factor[b], 0.0)
            for k in range(j + 1, GROUP):
                row = spread_row(col[k][b], j)
                for i in below:
                    col[k][i] = col[k][i] - factor[i] * row
            for h in range(halves):
                row = spread_row(x[b][h], j)
                for i in below:
                    x[i][h] = x[i][h] - factor[i] * row
            if b + 1 < groups:
                row = spread_row(g[b], j)
                for i in below:
                    g[i] = g[i] - factor[i] * row
        scale = lax.rsqrt(pivots)
        for h in range(halves):
            x[b][h] = x[b][h] * scale
    return jnp.concatenate([jnp.concatenate(parts, axis=1) for parts in x], axis=0)


def kernel(
    n, experts, count,
    grad, error, q_init,
    basis, q_out, new_error, norm,
    g_buf, e_buf, comb, fac0, fac, keep,
    s1_send, s1_recv, s2_send, s2_recv, p1, p1_recv, p2, n1, n2,
    g_sem, e_sem, q_sem, o_sem,
    s1_ss, s1_rs, s2_ss, s2_rs, p1_ss, p1_rs, p2_ss, p2_rs,
    ag_ss, fw_ss, ag_rs, n1_ss, n1_rs, n2_ss, n2_rs,
):
    me = lax.axis_index("dp")
    place = lax.axis_index("expert")
    chip, core = lax.div(me, 2), lax.rem(me, 2)
    partner = 2 * chip + 1 - core
    chips = n // 2
    rows, share = comb.shape[1], comb.shape[2]

    def send(src, dst, ssem, rsem, **where):
        return pltpu.make_async_remote_copy(
            src_ref=src, dst_ref=dst, send_sem=ssem, recv_sem=rsem, device_id=where, device_id_type=MESH
        )

    def columns(ref, j):
        return ref.at[:, pl.ds(pl.multiple_of(j * share, share), share)]

    def load(j):
        return (
            pltpu.make_async_copy(columns(grad, j), g_buf.at[j], g_sem.at[j]),
            pltpu.make_async_copy(columns(error, j), e_buf.at[j], e_sem.at[j]),
            pltpu.make_async_copy(columns(q_init, j), fac0.at[j], q_sem.at[j]),
        )

    for j in range(n):
        for copy in load(j):
            copy.start()

    barrier = pltpu.get_barrier_semaphore()
    for s in range(1, n):
        pl.semaphore_signal(barrier, inc=1, device_id={"dp": lax.rem(me + s, n)}, device_id_type=MESH)
    for s in range(1, experts):
        pl.semaphore_signal(
            barrier, inc=1, device_id={"expert": lax.rem(place + s, experts)}, device_id_type=MESH
        )

    def first(j, total):
        for copy in load(j):
            copy.wait()
        comb[j] = (g_buf[j].astype(F32) + e_buf[j].astype(F32)).astype(BF16)
        return total + lax.dot_general(fac0[j], comb[j], NT, preferred_element_type=F32)

    total = lax.fori_loop(0, n, first, jnp.zeros(p1.shape[1:], F32))
    pl.semaphore_wait(barrier, n - 1 + experts - 1)

    pending = []
    for it in range(ITERS):
        last = it == ITERS - 1
        p1[it] = total
        copy = send(p1.at[it], p1_recv.at[it], p1_ss.at[it], p1_rs.at[it], dp=partner)
        copy.start()
        pending.append(copy)
        copy.wait_recv()
        p2[it, chip] = p1[it] + p1_recv[it]
        copies = []
        for s in range(chips - 1, 0, -1):
            copies.append(
                send(
                    p2.at[it, chip], p2.at[it, chip], p2_ss.at[it, s], p2_rs.at[it, s],
                    dp=2 * xor(chip, s, chips) + core,
                )
            )
            copies[-1].start()
        for copy in copies:
            copy.wait_recv()
        pending += copies
        pt = p2[it, 0]
        for t in range(1, chips):
            pt = pt + p2[it, t]
        pt = pt / n
        ortho = orthonormal_rows(pt)
        low = ortho.astype(BF16)

        def finish(s):
            copy = first_hop[s]
            copy.wait_recv()
            both = keep[s] + s1_recv[it, s].astype(F32)
            if s == 0:
                return both
            s2_send[it, s] = both.astype(BF16)
            copy = send(
                s2_send.at[it, s], s2_recv.at[it, s], s2_ss.at[it, s], s2_rs.at[it, s],
                dp=2 * xor(chip, s, chips) + core,
            )
            copy.start()
            second_hop.append(copy)
            return None

        first_hop, second_hop = {}, []
        for s in range(chips - 1, -1, -1):
            t = xor(chip, s, chips)
            s1_send[it, s] = jnp.dot(
                low, comb[2 * t + 1 - core], preferred_element_type=F32
            ).astype(BF16)
            first_hop[s] = send(
                s1_send.at[it, s], s1_recv.at[it, s], s1_ss.at[it, s], s1_rs.at[it, s], dp=partner
            )
            first_hop[s].start()
            keep[s] = jnp.dot(low, comb[2 * t + core], preferred_element_type=F32)
            if s + 1 < chips:
                finish(s + 1)
        q = finish(0)
        if last:
            ortho_t = jnp.transpose(ortho)
            basis[...] = ortho_t
            low_t = ortho_t.astype(BF16)
        for copy in second_hop:
            copy.wait_recv()
        for s in range(1, chips):
            q = q + s2_recv[it, s].astype(F32)
        q = q / n
        pending += list(first_hop.values()) + second_hop
        if last:
            q_out[...] = q
        fac[it, me] = q.astype(BF16)

        for s in range(chips - 1, -1, -1):
            target = partner if s == 0 else 2 * xor(chip, s, chips) + core
            copy = send(fac.at[it, me], fac.at[it, me], ag_ss.at[it, s], ag_rs.at[it, me], dp=target)
            copy.start()
            pending.append(copy)

        def block(j, it=it):
            return fac.at[it, j]

        def arrived(j, it=it):
            send(fac.at[it, j], fac.at[it, j], fw_ss.at[it, 0], ag_rs.at[it, j], dp=partner).wait_recv()

        def forward(s, j, it=it):
            return send(fac.at[it, j], fac.at[it, j], fw_ss.at[it, s], ag_rs.at[it, j], dp=partner)

        if not last:
            def use(j, value, it=it):
                return value + lax.dot_general(fac[it, j], comb[j], NT, preferred_element_type=F32)

            value = jnp.zeros(p1.shape[1:], F32)
        else:
            def use(j, value, it=it):
                approx = jnp.dot(low_t, fac[it, j], preferred_element_type=F32)
                residual = (comb[j].astype(F32) - approx).astype(BF16)
                g_buf[j] = residual
                pltpu.make_async_copy(g_buf.at[j], columns(new_error, j), o_sem.at[j]).start()
                wide = residual.astype(F32)
                squares = jnp.sum((wide * wide).reshape(rows // GROUP, GROUP, share), axis=0)
                for h in range(share // LANES):
                    value = value + squares[:, LANES * h : LANES * (h + 1)]
                return value

            value = jnp.zeros(n1.shape[1:], F32)

        value = use(me, value)
        arrived(partner)
        value = use(partner, value)

        def step(s, value, use=use):
            t = xor(chip, s, chips)
            arrived(2 * t + core)
            forward(s, 2 * t + core).start()
            value = use(2 * t + core, value)
            arrived(2 * t + 1 - core)
            return use(2 * t + 1 - core, value)

        total = lax.fori_loop(1, chips, step, value)

    n1[me] = total
    copies = [
        send(n1.at[me], n1.at[me], n1_ss.at[s], n1_rs.at[s], dp=lax.rem(me + s, n)) for s in range(1, n)
    ]
    for copy in copies:
        copy.start()
    for copy in copies:
        copy.wait_recv()
    pending += copies
    total = n1[0]
    for j in range(1, n):
        total = total + n1[j]
    n2[place] = total
    copies = [
        send(n2.at[place], n2.at[place], n2_ss.at[s], n2_rs.at[s], expert=lax.rem(place + s, experts))
        for s in range(1, experts)
    ]
    for copy in copies:
        copy.start()
    for copy in copies:
        copy.wait_recv()
    pending += copies
    total = n2[0]
    for j in range(1, experts):
        total = total + n2[j]
    norm[...] = jnp.sqrt(jnp.sum(total, keepdims=True) / count)

    for copy in pending:
        copy.wait_send()
    for it in range(ITERS):
        for s in range(1, chips):
            j = 2 * xor(chip, s, chips) + core
            send(fac.at[it, j], fac.at[it, j], fw_ss.at[it, s], ag_rs.at[it, j], dp=partner).wait_send()
    for j in range(n):
        pltpu.make_async_copy(g_buf.at[j], columns(new_error, j), o_sem.at[j]).wait()


def local(grad, error, q_init):
    n, experts = lax.axis_size("dp"), lax.axis_size("expert")
    rows, width = grad.shape[2:]
    rank = q_init.shape[1]
    share = width // n
    chips = n // 2
    count = rows * width * n * experts
    dma = pltpu.SemaphoreType.DMA
    vmem, hbm = pl.BlockSpec(memory_space=pltpu.VMEM), pl.BlockSpec(memory_space=pl.ANY)
    hop = pltpu.VMEM((ITERS, chips, rank, share), BF16)
    basis, q, new_error, norm = pl.pallas_call(
        functools.partial(kernel, n, experts, count),
        out_shape=(
            jax.ShapeDtypeStruct((rows, rank), F32),
            jax.ShapeDtypeStruct((rank, share), F32),
            jax.ShapeDtypeStruct((rows, width), BF16),
            jax.ShapeDtypeStruct((1, 1), F32),
        ),
        in_specs=[hbm, hbm, hbm],
        out_specs=(vmem, vmem, hbm, vmem),
        scratch_shapes=[
            pltpu.VMEM((n, rows, share), BF16),
            pltpu.VMEM((n, rows, share), BF16),
            pltpu.VMEM((n, rows, share), BF16),
            pltpu.VMEM((n, rank, share), BF16),
            pltpu.VMEM((ITERS, n, rank, share), BF16),
            pltpu.VMEM((chips, rank, share), F32),
            hop, hop, hop, hop,
            pltpu.VMEM((ITERS, rank, rows), F32),
            pltpu.VMEM((ITERS, rank, rows), F32),
            pltpu.VMEM((ITERS, chips, rank, rows), F32),
            pltpu.VMEM((n, GROUP, LANES), F32),
            pltpu.VMEM((experts, GROUP, LANES), F32),
            dma((n,)), dma((n,)), dma((n,)), dma((n,)),
            dma((ITERS, chips)), dma((ITERS, chips)), dma((ITERS, chips)), dma((ITERS, chips)),
            dma((ITERS,)), dma((ITERS,)), dma((ITERS, chips)), dma((ITERS, chips)),
            dma((ITERS, chips)), dma((ITERS, chips)), dma((ITERS, n)),
            dma((n,)), dma((n,)), dma((experts,)), dma((experts,)),
        ],
        compiler_params=pltpu.CompilerParams(
            collective_id=0, has_side_effects=True, vmem_limit_bytes=56 * 2**20
        ),
        cost_estimate=pl.CostEstimate(
            flops=2 * 5 * rows * rank * width, bytes_accessed=6 * rows * width, transcendentals=0
        ),
    )(grad[0, 0], error[0, 0], q_init[0])
    return (basis[None], q[None], new_error[None, None], norm[0, 0])


def solution(mesh):
    placed = (P("expert", "dp", None, None), P("expert", "dp", None, None), P("expert", None, None))
    return jax.shard_map(
        local,
        mesh=mesh,
        in_specs=placed,
        out_specs=(
            P("expert", None, None),
            P("expert", None, "dp"),
            P("expert", "dp", None, None),
            P(),
        ),
        check_vma=False,
    )
```

time: 253 us -> 67.8 us (0.27)
  waiting for transfers between devices: 108 us -> 0 us
  blocking collectives: 87.3 us -> 0 us
  Pallas kernels: 0 us -> 57.3 us
  matrix products: 19.9 us -> 0 us
  other arithmetic: 18.5 us -> 0 us
  between operations: 16 us -> 2.46 us
  local copies, waits for them, and re-layouts: 2.84 us -> 7.8 us
    psum x2 -> x0, waiting for transfers between devices: 108 us -> none  [local(): lax.psum(right_part.astype(jnp.bfloat16), 'dp').astype(jnp.float32)]
    psum x3 -> x0, blocking collectives: 87.3 us -> none  [the longest x2 47.9 us: local(): projected = lax.psum(partial_value, 'dp') / replicas]
    pallas_call x0 -> x1, Pallas kernels: none -> 57.3 us  [local(): pl.pallas_call(functools.partial(kernel, n, experts, count), out_shape=(j...]
    dot_general x7 -> x0, matrix products: 19.4 us -> none  [the longest x2 7.68 us: local(): jnp.einsum('erk,erf->ekf', ortho_low, combined, preferred_element_type=jn...]
    another operation x10 -> x0, other arithmetic: 13.4 us -> none  [the longest x6 7.19 us: local(): lower_factor = jnp.linalg.cholesky(gram_of(projected))]
    unnamed x8 -> x3, local copies, waits for them, and re-layouts: 2.03 us -> 7.8 us
    convert_element_type x1 -> x0, other arithmetic: 5.06 us -> none  [local(): (grad[:, 0].astype(jnp.float32) + error[:, 0].astype(jnp.float32)).astype...]
  transfers between devices with their start and end apart: 2 -> 0, of which waited for: 2 -> 0; matrix products, arithmetic and copies ran while one was open for 0% -> 0% of each run, Pallas kernels for 0% -> 0%
where the time goes in v1:
time: 67.8 us; the launch traced here: 67.6 us
  Pallas kernels  57.3 us (85%)
  local copies, waits for them, and re-layouts  7.8 us (12%)
  between operations  2.46 us (4%)
    pallas_call x1, Pallas kernels, local(): pl.pallas_call(functools.partial(kernel, n, experts, count), out_shape=(j...  57.3 us
    unnamed x3, local copies, waits for them, and re-layouts  7.8 us

profile of v1, /device:TPU:0, one launch (start us, length us, event | category | flops | bytes accessed | tf_op | source)
XLA Modules:
  0.0 67.6 jit_solution(14678314561379758100)
XLA Ops:
  0.6 57.3 %shard_map.66 = (f32[256,32]{1,0:T(8,128)}, f32[32,1024]{1,0:T(8,128)}, bf16[256,8192]{1,0:T(8,128)(2,1)}, f32[1,1]{1,0:T(1,128)}) custom-call(bf16[256,8192]{1,0:T(8,128)(2,1)} %bitcast.7, bf16[256,8192]{1,0:T(8,128)(2,1)} %bitcast.8, bf16[32,8192]{1,0:T(8,128)(2,1)} %bitcast.10), custom_call_target="tpu_custom_call" | custom-call | flops 671088640 | bytes 12582912 | tf_op jit(solution)/shard_map/pallas_call | solution.py:292
  58.0 1.6 %copy.7 = f32[1,256,32]{1,2,0:T(8,128)} copy(f32[1,256,32]{2,1,0:T(8,128)} %bitcast.11) | data formatting | bytes 65536
  59.6 1.6 %copy.11 = f32[1,32,1024]{2,1,0:T(8,128)} copy(f32[1,32,1024]{2,1,0:T(8,128)} %bitcast.12) | data formatting | bytes 262144
  61.1 4.6 %copy.12 = bf16[1,1,256,8192]{3,2,1,0:T(8,128)(2,1)} copy(bf16[1,1,256,8192]{3,2,1,0:T(8,128)(2,1)} %bitcast.9) | data formatting | bytes 8388608

commit v2 on v1

--- a/solution.py
+++ b/solution.py
@@ -85,7 +85,7 @@
     chip, core = lax.div(me, 2), lax.rem(me, 2)
     partner = 2 * chip + 1 - core
     chips = n // 2
-    rows, share = comb.shape[1], comb.shape[2]
+    rows, share, rank = comb.shape[1], comb.shape[2], fac0.shape[1]
 
     def send(src, dst, ssem, rsem, **where):
         return pltpu.make_async_remote_copy(
@@ -118,15 +118,15 @@
         for copy in load(j):
             copy.wait()
         comb[j] = (g_buf[j].astype(F32) + e_buf[j].astype(F32)).astype(BF16)
-        return total + lax.dot_general(fac0[j], comb[j], NT, preferred_element_type=F32)
-
-    total = lax.fori_loop(0, n, first, jnp.zeros(p1.shape[1:], F32))
+        return total + lax.dot_general(comb[j], fac0[j], NT, preferred_element_type=F32)
+
+    total = lax.fori_loop(0, n, first, jnp.zeros((rows, rank), F32))
     pl.semaphore_wait(barrier, n - 1 + experts - 1)
 
     pending = []
     for it in range(ITERS):
         last = it == ITERS - 1
-        p1[it] = total
+        p1[it] = jnp.transpose(total)
         copy = send(p1.at[it], p1_recv.at[it], p1_ss.at[it], p1_rs.at[it], dp=partner)
         copy.start()
         pending.append(copy)
@@ -181,9 +181,8 @@
                 finish(s + 1)
         q = finish(0)
         if last:
-            ortho_t = jnp.transpose(ortho)
-            basis[...] = ortho_t
-            low_t = ortho_t.astype(BF16)
+            basis[...] = ortho
+            low_t = jnp.transpose(ortho).astype(BF16)
         for copy in second_hop:
             copy.wait_recv()
         for s in range(1, chips):
@@ -211,9 +210,9 @@
 
         if not last:
             def use(j, value, it=it):
-                return value + lax.dot_general(fac[it, j], comb[j], NT, preferred_element_type=F32)
-
-            value = jnp.zeros(p1.shape[1:], F32)
+                return value + lax.dot_general(comb[j], fac[it, j], NT, preferred_element_type=F32)
+
+            value = jnp.zeros((rows, rank), F32)
         else:
             def use(j, value, it=it):
                 approx = jnp.dot(low_t, fac[it, j], preferred_element_type=F32)
@@ -277,6 +276,35 @@
             send(fac.at[it, j], fac.at[it, j], fw_ss.at[it, s], ag_rs.at[it, j], dp=partner).wait_send()
     for j in range(n):
         pltpu.make_async_copy(g_buf.at[j], columns(new_error, j), o_sem.at[j]).wait()
+
+
+def hand_out_kernel(basis, q, new_error, basis_out, q_out, new_error_out, sems):
+    parts = sems.shape[0] - 2
+    height = new_error.shape[0] // parts
+    copies = [
+        pltpu.make_async_copy(
+            new_error.at[pl.ds(i * height, height), :], new_error_out.at[pl.ds(i * height, height), :], sems.at[i]
+        )
+        for i in range(parts)
+    ]
+    copies.append(pltpu.make_async_copy(basis, basis_out, sems.at[parts]))
+    copies.append(pltpu.make_async_copy(q, q_out, sems.at[parts + 1]))
+    for copy in copies:
+        copy.start()
+    for copy in copies:
+        copy.wait()
+
+
+def hand_out(*arrays):
+    hbm = pl.BlockSpec(memory_space=pl.ANY)
+    return pl.pallas_call(
+        hand_out_kernel,
+        out_shape=tuple(jax.ShapeDtypeStruct(a.shape, a.dtype) for a in arrays),
+        in_specs=[hbm] * 3,
+        out_specs=(hbm,) * 3,
+        scratch_shapes=[pltpu.SemaphoreType.DMA((16 + 2,))],
+        compiler_params=pltpu.CompilerParams(vmem_limit_bytes=60 * 2**20),
+    )(*arrays)
 
 
 def local(grad, error, q_init):
@@ -292,7 +320,7 @@
     basis, q, new_error, norm = pl.pallas_call(
         functools.partial(kernel, n, experts, count),
         out_shape=(
-            jax.ShapeDtypeStruct((rows, rank), F32),
+            jax.ShapeDtypeStruct((rank, rows), F32),
             jax.ShapeDtypeStruct((rank, share), F32),
             jax.ShapeDtypeStruct((rows, width), BF16),
             jax.ShapeDtypeStruct((1, 1), F32),
@@ -325,7 +353,8 @@
             flops=2 * 5 * rows * rank * width, bytes_accessed=6 * rows * width, transcendentals=0
         ),
     )(grad[0, 0], error[0, 0], q_init[0])
-    return (basis[None], q[None], new_error[None, None], norm[0, 0])
+    basis, q, new_error = hand_out(basis, q, new_error)
+    return (jnp.transpose(basis)[None], q[None], new_error[None, None], norm[0, 0])
 
 
 def solution(mesh):

time: 67.8 us -> 193 us (2.85)
  Pallas kernels: 57.3 us -> 191 us
  local copies, waits for them, and re-layouts: 7.8 us -> 0 us
    pallas_call x0 -> x1, Pallas kernels: none -> 133 us  [hand_out(): pl.pallas_call(hand_out_kernel, out_shape=tuple((jax.ShapeDtypeStruct(a.s...]
    unnamed x3 -> x0, local copies, waits for them, and re-layouts: 7.8 us -> none
where the time goes in v2:
time: 193 us
  Pallas kernels  191 us (99%)
  between operations  2.35 us (1%)
    pallas_call x1, Pallas kernels, hand_out(): pl.pallas_call(hand_out_kernel, out_shape=tuple((jax.ShapeDtypeStruct(a.s...  133 us
    pallas_call x1, Pallas kernels, local(): pl.pallas_call(functools.partial(kernel, n, experts, count), out_shape=(j...  57.5 us

profile of v2, /device:TPU:0, one launch (start us, length us, event | category | flops | bytes accessed | tf_op | source)
XLA Modules:
  0.0 193.1 jit_solution(12760293016258005718)
XLA Ops:
  0.6 57.5 %shard_map.66 = (f32[32,256]{1,0:T(8,128)}, f32[32,1024]{1,0:T(8,128)}, bf16[256,8192]{1,0:T(8,128)(2,1)}, f32[1,1]{1,0:T(1,128)}) custom-call(bf16[256,8192]{1,0:T(8,128)(2,1)} %bitcast.9, bf16[256,8192]{1,0:T(8,128)(2,1)} %bitcast.10, bf16[32,8192]{1,0:T(8,128)(2,1)} %bitcast.11), custom_call_target="tpu_custom_call" | custom-call | flops 671088640 | bytes 12582912 | tf_op jit(solution)/shard_map/pallas_call | solution.py:320
  58.1 133.3 %shard_map.67 = (f32[32,256]{1,0:T(8,128)}, f32[32,1024]{1,0:T(8,128)}, bf16[256,8192]{1,0:T(8,128)(2,1)}) custom-call(f32[32,256]{1,0:T(8,128)} %get-tuple-element.11.basis, f32[32,1024]{1,0:T(8,128)} %get-tuple-element.12.q, bf16[256,8192]{1,0:T(8,128)(2,1)} %get-tuple-element.13.new_error), custom_call_target="tpu_custom_call" | custom-call | tf_op jit(solution)/shard_map/pallas_call | solution.py:300

commit v3 on v2

--- a/solution.py
+++ b/solution.py
@@ -74,8 +74,8 @@
     n, experts, count,
     grad, error, q_init,
     basis, q_out, new_error, norm,
-    g_buf, e_buf, comb, fac0, fac, keep,
-    s1_send, s1_recv, s2_send, s2_recv, p1, p1_recv, p2, n1, n2,
+    g_buf, e_buf, comb, theirs, pair, fac0, fac,
+    s2_send, s2_recv, p1, p1_recv, p2, n1, n2,
     g_sem, e_sem, q_sem, o_sem,
     s1_ss, s1_rs, s2_ss, s2_rs, p1_ss, p1_rs, p2_ss, p2_rs,
     ag_ss, fw_ss, ag_rs, n1_ss, n1_rs, n2_ss, n2_rs,
@@ -99,12 +99,26 @@
         return (
             pltpu.make_async_copy(columns(grad, j), g_buf.at[j], g_sem.at[j]),
             pltpu.make_async_copy(columns(error, j), e_buf.at[j], e_sem.at[j]),
-            pltpu.make_async_copy(columns(q_init, j), fac0.at[j], q_sem.at[j]),
         )
 
-    for j in range(n):
+    def load_factor(t):
+        return pltpu.make_async_copy(columns(q_init, 2 * t + core), fac0.at[t], q_sem.at[t])
+
+    def combine(j):
         for copy in load(j):
+            copy.wait()
+        comb[j] = (g_buf[j].astype(F32) + e_buf[j].astype(F32)).astype(BF16)
+
+    def hand_over(t):
+        return send(comb.at[2 * t + 1 - core], theirs.at[t], s1_ss.at[t], s1_rs.at[t], dp=partner)
+
+    for t in range(chips):
+        for copy in load(2 * t + 1 - core):
             copy.start()
+    for t in range(chips):
+        for copy in load(2 * t + core):
+            copy.start()
+        load_factor(t).start()
 
     barrier = pltpu.get_barrier_semaphore()
     for s in range(1, n):
@@ -114,14 +128,25 @@
             barrier, inc=1, device_id={"expert": lax.rem(place + s, experts)}, device_id_type=MESH
         )
 
-    def first(j, total):
-        for copy in load(j):
-            copy.wait()
-        comb[j] = (g_buf[j].astype(F32) + e_buf[j].astype(F32)).astype(BF16)
-        return total + lax.dot_general(comb[j], fac0[j], NT, preferred_element_type=F32)
-
-    total = lax.fori_loop(0, n, first, jnp.zeros((rows, rank), F32))
+    combine(1 - core)
     pl.semaphore_wait(barrier, n - 1 + experts - 1)
+    hand_over(0).start()
+
+    def first(t, _):
+        combine(2 * t + 1 - core)
+        hand_over(t).start()
+        return 0
+
+    lax.fori_loop(1, chips, first, 0)
+
+    def second(t, total):
+        combine(2 * t + core)
+        load_factor(t).wait()
+        hand_over(t).wait_recv()
+        pair[t] = (comb[2 * t + core].astype(F32) + theirs[t].astype(F32)).astype(BF16)
+        return total + lax.dot_general(pair[t], fac0[t], NT, preferred_element_type=F32)
+
+    total = lax.fori_loop(0, chips, second, jnp.zeros((rows, rank), F32))
 
     pending = []
     for it in range(ITERS):
@@ -151,35 +176,18 @@
         ortho = orthonormal_rows(pt)
         low = ortho.astype(BF16)
 
-        def finish(s):
-            copy = first_hop[s]
-            copy.wait_recv()
-            both = keep[s] + s1_recv[it, s].astype(F32)
-            if s == 0:
-                return both
-            s2_send[it, s] = both.astype(BF16)
-            copy = send(
-                s2_send.at[it, s], s2_recv.at[it, s], s2_ss.at[it, s], s2_rs.at[it, s],
-                dp=2 * xor(chip, s, chips) + core,
-            )
-            copy.start()
-            second_hop.append(copy)
-            return None
-
-        first_hop, second_hop = {}, []
+        second_hop = []
         for s in range(chips - 1, -1, -1):
-            t = xor(chip, s, chips)
-            s1_send[it, s] = jnp.dot(
-                low, comb[2 * t + 1 - core], preferred_element_type=F32
-            ).astype(BF16)
-            first_hop[s] = send(
-                s1_send.at[it, s], s1_recv.at[it, s], s1_ss.at[it, s], s1_rs.at[it, s], dp=partner
-            )
-            first_hop[s].start()
-            keep[s] = jnp.dot(low, comb[2 * t + core], preferred_element_type=F32)
-            if s + 1 < chips:
-                finish(s + 1)
-        q = finish(0)
+            q = jnp.dot(low, pair[xor(chip, s, chips)], preferred_element_type=F32)
+            if s:
+                s2_send[it, s] = q.astype(BF16)
+                second_hop.append(
+                    send(
+                        s2_send.at[it, s], s2_recv.at[it, s], s2_ss.at[it, s], s2_rs.at[it, s],
+                        dp=2 * xor(chip, s, chips) + core,
+                    )
+                )
+                second_hop[-1].start()
         if last:
             basis[...] = ortho
             low_t = jnp.transpose(ortho).astype(BF16)
@@ -188,31 +196,33 @@
         for s in range(1, chips):
             q = q + s2_recv[it, s].astype(F32)
         q = q / n
-        pending += list(first_hop.values()) + second_hop
+        pending += second_hop
         if last:
             q_out[...] = q
         fac[it, me] = q.astype(BF16)
 
-        for s in range(chips - 1, -1, -1):
+        for s in range(chips - 1, -1 if last else 0, -1):
             target = partner if s == 0 else 2 * xor(chip, s, chips) + core
             copy = send(fac.at[it, me], fac.at[it, me], ag_ss.at[it, s], ag_rs.at[it, me], dp=target)
             copy.start()
             pending.append(copy)
 
-        def block(j, it=it):
-            return fac.at[it, j]
-
-        def arrived(j, it=it):
-            send(fac.at[it, j], fac.at[it, j], fw_ss.at[it, 0], ag_rs.at[it, j], dp=partner).wait_recv()
-
         def forward(s, j, it=it):
-            return send(fac.at[it, j], fac.at[it, j], fw_ss.at[it, s], ag_rs.at[it, j], dp=partner)
+            return send(fac.at[it, j], fac.at[it, j], fw_ss.at[s], ag_rs.at[it, j], dp=partner)
+
+        def arrived(j):
+            forward(0, j).wait_recv()
 
         if not last:
-            def use(j, value, it=it):
-                return value + lax.dot_general(comb[j], fac[it, j], NT, preferred_element_type=F32)
-
-            value = jnp.zeros((rows, rank), F32)
+            def use(t, value, it=it):
+                return value + lax.dot_general(pair[t], fac[it, 2 * t + core], NT, preferred_element_type=F32)
+
+            def step(s, value):
+                t = xor(chip, s, chips)
+                arrived(2 * t + core)
+                return use(t, value)
+
+            value = use(chip, jnp.zeros((rows, rank), F32))
         else:
             def use(j, value, it=it):
                 approx = jnp.dot(low_t, fac[it, j], preferred_element_type=F32)
@@ -225,19 +235,17 @@
                     value = value + squares[:, LANES * h : LANES * (h + 1)]
                 return value
 
-            value = jnp.zeros(n1.shape[1:], F32)
-
-        value = use(me, value)
-        arrived(partner)
-        value = use(partner, value)
-
-        def step(s, value, use=use):
-            t = xor(chip, s, chips)
-            arrived(2 * t + core)
-            forward(s, 2 * t + core).start()
-            value = use(2 * t + core, value)
-            arrived(2 * t + 1 - core)
-            return use(2 * t + 1 - core, value)
+            def step(s, value):
+                t = xor(chip, s, chips)
+                arrived(2 * t + core)
+                forward(s, 2 * t + core).start()
+                value = use(2 * t + core, value)
+                arrived(2 * t + 1 - core)
+                return use(2 * t + 1 - core, value)
+
+            value = use(me, jnp.zeros(n1.shape[1:], F32))
+            arrived(partner)
+            value = use(partner, value)
 
         total = lax.fori_loop(1, chips, step, value)
 
@@ -270,28 +278,31 @@
 
     for copy in pending:
         copy.wait_send()
-    for it in range(ITERS):
-        for s in range(1, chips):
-            j = 2 * xor(chip, s, chips) + core
-            send(fac.at[it, j], fac.at[it, j], fw_ss.at[it, s], ag_rs.at[it, j], dp=partner).wait_send()
+    for s in range(1, chips):
+        forward(s, 2 * xor(chip, s, chips) + core).wait_send()
+    for t in range(chips):
+        hand_over(t).wait_send()
     for j in range(n):
         pltpu.make_async_copy(g_buf.at[j], columns(new_error, j), o_sem.at[j]).wait()
 
 
-def hand_out_kernel(basis, q, new_error, basis_out, q_out, new_error_out, sems):
-    parts = sems.shape[0] - 2
+def hand_out_kernel(basis, q, new_error, basis_out, q_out, new_error_out, b_buf, q_buf, e_buf, in_sem, out_sem):
+    parts = in_sem.shape[0] - 2
     height = new_error.shape[0] // parts
-    copies = [
-        pltpu.make_async_copy(
-            new_error.at[pl.ds(i * height, height), :], new_error_out.at[pl.ds(i * height, height), :], sems.at[i]
-        )
-        for i in range(parts)
-    ]
-    copies.append(pltpu.make_async_copy(basis, basis_out, sems.at[parts]))
-    copies.append(pltpu.make_async_copy(q, q_out, sems.at[parts + 1]))
-    for copy in copies:
+
+    def piece(ref, i):
+        return ref.at[pl.ds(i * height, height), :]
+
+    moves = [(piece(new_error, i), piece(e_buf, i), piece(new_error_out, i)) for i in range(parts)]
+    moves += [(basis, b_buf, basis_out), (q, q_buf, q_out)]
+    inward = [pltpu.make_async_copy(a, b, in_sem.at[i]) for i, (a, b, c) in enumerate(moves)]
+    outward = [pltpu.make_async_copy(b, c, out_sem.at[i]) for i, (a, b, c) in enumerate(moves)]
+    for copy in inward:
         copy.start()
-    for copy in copies:
+    for copy, following in zip(inward, outward):
+        copy.wait()
+        following.start()
+    for copy in outward:
         copy.wait()
 
 
@@ -302,7 +313,7 @@
         out_shape=tuple(jax.ShapeDtypeStruct(a.shape, a.dtype) for a in arrays),
         in_specs=[hbm] * 3,
         out_specs=(hbm,) * 3,
-        scratch_shapes=[pltpu.SemaphoreType.DMA((16 + 2,))],
+        scratch_shapes=[pltpu.VMEM(a.shape, a.dtype) for a in arrays] + [pltpu.SemaphoreType.DMA((16 + 2,))] * 2,
         compiler_params=pltpu.CompilerParams(vmem_limit_bytes=60 * 2**20),
     )(*arrays)
 
@@ -331,19 +342,20 @@
             pltpu.VMEM((n, rows, share), BF16),
             pltpu.VMEM((n, rows, share), BF16),
             pltpu.VMEM((n, rows, share), BF16),
-            pltpu.VMEM((n, rank, share), BF16),
+            pltpu.VMEM((chips, rows, share), BF16),
+            pltpu.VMEM((chips, rows, share), BF16),
+            pltpu.VMEM((chips, rank, share), BF16),
             pltpu.VMEM((ITERS, n, rank, share), BF16),
-            pltpu.VMEM((chips, rank, share), F32),
-            hop, hop, hop, hop,
+            hop, hop,
             pltpu.VMEM((ITERS, rank, rows), F32),
             pltpu.VMEM((ITERS, rank, rows), F32),
             pltpu.VMEM((ITERS, chips, rank, rows), F32),
             pltpu.VMEM((n, GROUP, LANES), F32),
             pltpu.VMEM((experts, GROUP, LANES), F32),
-            dma((n,)), dma((n,)), dma((n,)), dma((n,)),
-            dma((ITERS, chips)), dma((ITERS, chips)), dma((ITERS, chips)), dma((ITERS, chips)),
+            dma((n,)), dma((n,)), dma((chips,)), dma((n,)),
+            dma((chips,)), dma((chips,)), dma((ITERS, chips)), dma((ITERS, chips)),
             dma((ITERS,)), dma((ITERS,)), dma((ITERS, chips)), dma((ITERS, chips)),
-            dma((ITERS, chips)), dma((ITERS, chips)), dma((ITERS, n)),
+            dma((ITERS, chips)), dma((chips,)), dma((ITERS, n)),
             dma((n,)), dma((n,)), dma((experts,)), dma((experts,)),
         ],
         compiler_params=pltpu.CompilerParams(

time: 193 us -> 58.1 us (0.30)
  Pallas kernels: 191 us -> 55.6 us
    pallas_call x1, Pallas kernels: 133 us -> 4 us  [hand_out(): pl.pallas_call(hand_out_kernel, out_shape=tuple((jax.ShapeDtypeStruct(a.s...]
    pallas_call x1, Pallas kernels: 57.5 us -> 51.6 us  [local(): pl.pallas_call(functools.partial(kernel, n, experts, count), out_shape=(j...]
where the time goes in v3:
time: 58.1 us; the launch traced here: 58 us
  Pallas kernels  55.6 us (96%)
  between operations  2.35 us (4%)
    pallas_call x1, Pallas kernels, local(): pl.pallas_call(functools.partial(kernel, n, experts, count), out_shape=(j...  51.6 us
    pallas_call x1, Pallas kernels, hand_out(): pl.pallas_call(hand_out_kernel, out_shape=tuple((jax.ShapeDtypeStruct(a.s...  4 us

profile of v3, /device:TPU:0, one launch (start us, length us, event | category | flops | bytes accessed | tf_op | source)
XLA Modules:
  0.0 58.0 jit_solution(17004046699081996545)
XLA Ops:
  0.6 51.6 %shard_map.66 = (f32[32,256]{1,0:T(8,128)}, f32[32,1024]{1,0:T(8,128)}, bf16[256,8192]{1,0:T(8,128)(2,1)}, f32[1,1]{1,0:T(1,128)}) custom-call(bf16[256,8192]{1,0:T(8,128)(2,1)} %bitcast.9, bf16[256,8192]{1,0:T(8,128)(2,1)} %bitcast.10, bf16[32,8192]{1,0:T(8,128)(2,1)} %bitcast.11), custom_call_target="tpu_custom_call" | custom-call | flops 671088640 | bytes 12582912 | tf_op jit(solution)/shard_map/pallas_call | solution.py:331
  52.2 4.0 %shard_map.67 = (f32[32,256]{1,0:T(8,128)}, f32[32,1024]{1,0:T(8,128)}, bf16[256,8192]{1,0:T(8,128)(2,1)}) custom-call(f32[32,256]{1,0:T(8,128)} %get-tuple-element.11.basis, f32[32,1024]{1,0:T(8,128)} %get-tuple-element.12.q, bf16[256,8192]{1,0:T(8,128)(2,1)} %get-tuple-element.13.new_error), custom_call_target="tpu_custom_call" | custom-call | tf_op jit(solution)/shard_map/pallas_call | solution.py:311

commit v4 on v3

--- a/solution.py
+++ b/solution.py
@@ -26,6 +26,13 @@
 
 def spread_row(tile, j):
     return jnp.broadcast_to(tile[j : j + 1, :], tile.shape)
+
+
+def inverted(x):
+    guess = pl.reciprocal(x, approx=True)
+    for _ in range(2):
+        guess = guess * (2.0 - x * guess)
+    return guess
 
 
 def orthonormal_rows(pt):
@@ -45,17 +52,21 @@
             {i: jnp.broadcast_to(g[i][:, GROUP * b + j : GROUP * b + j + 1], (GROUP, LANES)) for i in below}
             for j in range(GROUP)
         ]
+        entry = {(j, k): spread_row(col[k][b], j) for j in range(GROUP) for k in range(j, GROUP)}
         pivots = jnp.ones((GROUP, LANES), F32)
         for j in range(GROUP):
-            pivot = spread_row(col[j][b], j)
+            pivot = entry[j, j]
             pivots = jnp.where(row_id == j, pivot, pivots)
-            inverse = 1.0 / pivot
+            inverse = inverted(pivot)
+            for k in range(j + 1, GROUP):
+                ratio = entry[j, k] * inverse
+                for l in range(k, GROUP):
+                    entry[k, l] = entry[k, l] - ratio * entry[j, l]
             factor = {i: col[j][i] * inverse for i in below}
             factor[b] = jnp.where(row_id > j, factor[b], 0.0)
             for k in range(j + 1, GROUP):
-                row = spread_row(col[k][b], j)
                 for i in below:
-                    col[k][i] = col[k][i] - factor[i] * row
+                    col[k][i] = col[k][i] - factor[i] * entry[j, k]
             for h in range(halves):
                 row = spread_row(x[b][h], j)
                 for i in below:
@@ -286,23 +297,19 @@
         pltpu.make_async_copy(g_buf.at[j], columns(new_error, j), o_sem.at[j]).wait()
 
 
-def hand_out_kernel(basis, q, new_error, basis_out, q_out, new_error_out, b_buf, q_buf, e_buf, in_sem, out_sem):
-    parts = in_sem.shape[0] - 2
+def hand_out_kernel(basis, q, new_error, basis_out, q_out, new_error_out, sem):
+    parts = sem.shape[0] - 2
     height = new_error.shape[0] // parts
 
     def piece(ref, i):
         return ref.at[pl.ds(i * height, height), :]
 
-    moves = [(piece(new_error, i), piece(e_buf, i), piece(new_error_out, i)) for i in range(parts)]
-    moves += [(basis, b_buf, basis_out), (q, q_buf, q_out)]
-    inward = [pltpu.make_async_copy(a, b, in_sem.at[i]) for i, (a, b, c) in enumerate(moves)]
-    outward = [pltpu.make_async_copy(b, c, out_sem.at[i]) for i, (a, b, c) in enumerate(moves)]
-    for copy in inward:
+    moves = [(piece(new_error, i), piece(new_error_out, i)) for i in range(parts)]
+    moves += [(basis, basis_out), (q, q_out)]
+    copies = [pltpu.make_async_copy(a, b, sem.at[i]) for i, (a, b) in enumerate(moves)]
+    for copy in copies:
         copy.start()
-    for copy, following in zip(inward, outward):
-        copy.wait()
-        following.start()
-    for copy in outward:
+    for copy in copies:
         copy.wait()
 
 
@@ -313,8 +320,8 @@
         out_shape=tuple(jax.ShapeDtypeStruct(a.shape, a.dtype) for a in arrays),
         in_specs=[hbm] * 3,
         out_specs=(hbm,) * 3,
-        scratch_shapes=[pltpu.VMEM(a.shape, a.dtype) for a in arrays] + [pltpu.SemaphoreType.DMA((16 + 2,))] * 2,
-        compiler_params=pltpu.CompilerParams(vmem_limit_bytes=60 * 2**20),
+        scratch_shapes=[pltpu.SemaphoreType.DMA((16 + 2,))],
+        compiler_params=pltpu.CompilerParams(vmem_limit_bytes=32 * 2**20),
     )(*arrays)
 
 
@@ -359,7 +366,7 @@
             dma((n,)), dma((n,)), dma((experts,)), dma((experts,)),
         ],
         compiler_params=pltpu.CompilerParams(
-            collective_id=0, has_side_effects=True, vmem_limit_bytes=56 * 2**20
+            collective_id=0, has_side_effects=True, vmem_limit_bytes=49 * 2**20
         ),
         cost_estimate=pl.CostEstimate(
             flops=2 * 5 * rows * rank * width, bytes_accessed=6 * rows * width, transcendentals=0

time: 58.1 us -> 58.2 us (level)
  local copies, waits for them, and re-layouts: 0 us -> 1.03 us
  Pallas kernels: 55.6 us -> 54.6 us
    pallas_call x1, Pallas kernels: 4 us -> 2.2 us  [hand_out(): pl.pallas_call(hand_out_kernel, out_shape=tuple((jax.ShapeDtypeStruct(a.s...]
    unnamed x0 -> x2, local copies, waits for them, and re-layouts: none -> 1.03 us
    pallas_call x1, Pallas kernels: 51.6 us -> 52.4 us  [local(): pl.pallas_call(functools.partial(kernel, n, experts, count), out_shape=(j...]
where the time goes in v4:
time: 58.2 us; the launch traced here: 58 us
  Pallas kernels  54.6 us (94%)
  between operations  2.41 us (4%)
  local copies, waits for them, and re-layouts  1.03 us (2%)
    pallas_call x1, Pallas kernels, local(): pl.pallas_call(functools.partial(kernel, n, experts, count), out_shape=(j...  52.4 us
    pallas_call x1, Pallas kernels, hand_out(): pl.pallas_call(hand_out_kernel, out_shape=tuple((jax.ShapeDtypeStruct(a.s...  2.2 us

profile of v4, /device:TPU:0, one launch (start us, length us, event | category | flops | bytes accessed | tf_op | source)
XLA Modules:
  0.0 58.0 jit_solution(11179724770868779619)
XLA Ops:
  0.6 0.0 copy-start
  0.6 1.0 %copy-done = bf16[1,32,8192]{2,1,0:T(8,128)(2,1)S(1)} copy-done((bf16[1,32,8192]{2,1,0:T(8,128)(2,1)S(1)}, bf16[1,32,8192]{2,1,0:T(8,128)(2,1)}, u32[]{:S(2)}) %copy-start) | copy-done | bytes 524312
  1.7 52.4 %shard_map.66 = (f32[32,256]{1,0:T(8,128)S(1)}, f32[32,1024]{1,0:T(8,128)S(1)}, bf16[256,8192]{1,0:T(8,128)(2,1)S(1)}, f32[1,1]{1,0:T(1,128)}) custom-call(bf16[256,8192]{1,0:T(8,128)(2,1)} %bitcast.10, bf16[256,8192]{1,0:T(8,128)(2,1)} %bitcast.11, bf16[32,8192]{1,0:T(8,128)(2,1)S(1)} %bitcast.9), custom_call_target="tpu_custom_call" | custom-call | flops 671088640 | bytes 12582912 | tf_op jit(solution)/shard_map/pallas_call | solution.py:338
  54.0 2.2 %shard_map.67 = (f32[32,256]{1,0:T(8,128)}, f32[32,1024]{1,0:T(8,128)}, bf16[256,8192]{1,0:T(8,128)(2,1)}) custom-call(f32[32,256]{1,0:T(8,128)S(1)} %get-tuple-element.11.basis, f32[32,1024]{1,0:T(8,128)S(1)} %get-tuple-element.12.q, bf16[256,8192]{1,0:T(8,128)(2,1)S(1)} %get-tuple-element.13.new_error), custom_call_target="tpu_custom_call" | custom-call | tf_op jit(solution)/shard_map/pallas_call | solution.py:318
Async XLA Ops:
  0.6 1.0 %copy-start = (bf16[1,32,8192]{2,1,0:T(8,128)(2,1)S(1)}, bf16[1,32,8192]{2,1,0:T(8,128)(2,1)}, u32[]{:S(2)}) copy-start(bf16[1,32,8192]{2,1,0:T(8,128)(2,1)} %param.5) | copy-start | bytes 1572868

commit v5 on v4

--- a/solution.py
+++ b/solution.py
@@ -26,13 +26,6 @@
 
 def spread_row(tile, j):
     return jnp.broadcast_to(tile[j : j + 1, :], tile.shape)
-
-
-def inverted(x):
-    guess = pl.reciprocal(x, approx=True)
-    for _ in range(2):
-        guess = guess * (2.0 - x * guess)
-    return guess
 
 
 def orthonormal_rows(pt):
@@ -52,21 +45,17 @@
             {i: jnp.broadcast_to(g[i][:, GROUP * b + j : GROUP * b + j + 1], (GROUP, LANES)) for i in below}
             for j in range(GROUP)
         ]
-        entry = {(j, k): spread_row(col[k][b], j) for j in range(GROUP) for k in range(j, GROUP)}
         pivots = jnp.ones((GROUP, LANES), F32)
         for j in range(GROUP):
-            pivot = entry[j, j]
+            pivot = spread_row(col[j][b], j)
             pivots = jnp.where(row_id == j, pivot, pivots)
-            inverse = inverted(pivot)
-            for k in range(j + 1, GROUP):
-                ratio = entry[j, k] * inverse
-                for l in range(k, GROUP):
-                    entry[k, l] = entry[k, l] - ratio * entry[j, l]
+            inverse = 1.0 / pivot
             factor = {i: col[j][i] * inverse for i in below}
             factor[b] = jnp.where(row_id > j, factor[b], 0.0)
             for k in range(j + 1, GROUP):
+                row = spread_row(col[k][b], j)
                 for i in below:
-                    col[k][i] = col[k][i] - factor[i] * entry[j, k]
+                    col[k][i] = col[k][i] - factor[i] * row
             for h in range(halves):
                 row = spread_row(x[b][h], j)
                 for i in below:
@@ -86,9 +75,9 @@
     grad, error, q_init,
     basis, q_out, new_error, norm,
     g_buf, e_buf, comb, theirs, pair, fac0, fac,
-    s2_send, s2_recv, p1, p1_recv, p2, n1, n2,
+    s2_send, s2_recv, p, n1, n2,
     g_sem, e_sem, q_sem, o_sem,
-    s1_ss, s1_rs, s2_ss, s2_rs, p1_ss, p1_rs, p2_ss, p2_rs,
+    s1_ss, s1_rs, s2_ss, s2_rs, p_ss, p_rs,
     ag_ss, fw_ss, ag_rs, n1_ss, n1_rs, n2_ss, n2_rs,
 ):
     me = lax.axis_index("dp")
@@ -110,15 +99,14 @@
         return (
             pltpu.make_async_copy(columns(grad, j), g_buf.at[j], g_sem.at[j]),
             pltpu.make_async_copy(columns(error, j), e_buf.at[j], e_sem.at[j]),
+            pltpu.make_async_copy(columns(q_init, j), fac0.at[j], q_sem.at[j]),
         )
 
-    def load_factor(t):
-        return pltpu.make_async_copy(columns(q_init, 2 * t + core), fac0.at[t], q_sem.at[t])
-
-    def combine(j):
+    def combine(j, total):
         for copy in load(j):
             copy.wait()
         comb[j] = (g_buf[j].astype(F32) + e_buf[j].astype(F32)).astype(BF16)
+        return total + lax.dot_general(comb[j], fac0[j], NT, preferred_element_type=F32)
 
     def hand_over(t):
         return send(comb.at[2 * t + 1 - core], theirs.at[t], s1_ss.at[t], s1_rs.at[t], dp=partner)
@@ -129,7 +117,6 @@
     for t in range(chips):
         for copy in load(2 * t + core):
             copy.start()
-        load_factor(t).start()
 
     barrier = pltpu.get_barrier_semaphore()
     for s in range(1, n):
@@ -139,50 +126,41 @@
             barrier, inc=1, device_id={"expert": lax.rem(place + s, experts)}, device_id_type=MESH
         )
 
-    combine(1 - core)
+    total = combine(1 - core, jnp.zeros((rows, rank), F32))
     pl.semaphore_wait(barrier, n - 1 + experts - 1)
     hand_over(0).start()
 
-    def first(t, _):
-        combine(2 * t + 1 - core)
+    def first(t, total):
+        total = combine(2 * t + 1 - core, total)
         hand_over(t).start()
-        return 0
-
-    lax.fori_loop(1, chips, first, 0)
-
-    def second(t, total):
-        combine(2 * t + core)
-        load_factor(t).wait()
+        return total
+
+    total = lax.fori_loop(1, chips, first, total)
+    total = lax.fori_loop(0, chips, lambda t, total: combine(2 * t + core, total), total)
+
+    def add_pair(t, _):
         hand_over(t).wait_recv()
         pair[t] = (comb[2 * t + core].astype(F32) + theirs[t].astype(F32)).astype(BF16)
-        return total + lax.dot_general(pair[t], fac0[t], NT, preferred_element_type=F32)
-
-    total = lax.fori_loop(0, chips, second, jnp.zeros((rows, rank), F32))
+        return 0
 
     pending = []
     for it in range(ITERS):
         last = it == ITERS - 1
-        p1[it] = jnp.transpose(total)
-        copy = send(p1.at[it], p1_recv.at[it], p1_ss.at[it], p1_rs.at[it], dp=partner)
-        copy.start()
-        pending.append(copy)
-        copy.wait_recv()
-        p2[it, chip] = p1[it] + p1_recv[it]
+        p[it, me] = jnp.transpose(total).astype(BF16)
         copies = []
-        for s in range(chips - 1, 0, -1):
+        for s in range(n - 1, 0, -1):
             copies.append(
-                send(
-                    p2.at[it, chip], p2.at[it, chip], p2_ss.at[it, s], p2_rs.at[it, s],
-                    dp=2 * xor(chip, s, chips) + core,
-                )
+                send(p.at[it, me], p.at[it, me], p_ss.at[it, s], p_rs.at[it, s], dp=xor(me, s, n))
             )
             copies[-1].start()
+        if it == 0:
+            lax.fori_loop(0, chips, add_pair, 0)
         for copy in copies:
             copy.wait_recv()
         pending += copies
-        pt = p2[it, 0]
-        for t in range(1, chips):
-            pt = pt + p2[it, t]
+        pt = p[it, 0].astype(F32)
+        for j in range(1, n):
+            pt = pt + p[it, j].astype(F32)
         pt = pt / n
         ortho = orthonormal_rows(pt)
         low = ortho.astype(BF16)
@@ -351,17 +329,15 @@
             pltpu.VMEM((n, rows, share), BF16),
             pltpu.VMEM((chips, rows, share), BF16),
             pltpu.VMEM((chips, rows, share), BF16),
-            pltpu.VMEM((chips, rank, share), BF16),
+            pltpu.VMEM((n, rank, share), BF16),
             pltpu.VMEM((ITERS, n, rank, share), BF16),
             hop, hop,
-            pltpu.VMEM((ITERS, rank, rows), F32),
-            pltpu.VMEM((ITERS, rank, rows), F32),
-            pltpu.VMEM((ITERS, chips, rank, rows), F32),
+            pltpu.VMEM((ITERS, n, rank, rows), BF16),
             pltpu.VMEM((n, GROUP, LANES), F32),
             pltpu.VMEM((experts, GROUP, LANES), F32),
-            dma((n,)), dma((n,)), dma((chips,)), dma((n,)),
+            dma((n,)), dma((n,)), dma((n,)), dma((n,)),
             dma((chips,)), dma((chips,)), dma((ITERS, chips)), dma((ITERS, chips)),
-            dma((ITERS,)), dma((ITERS,)), dma((ITERS, chips)), dma((ITERS, chips)),
+            dma((ITERS, n)), dma((ITERS, n)),
             dma((ITERS, chips)), dma((chips,)), dma((ITERS, n)),
             dma((n,)), dma((n,)), dma((experts,)), dma((experts,)),
         ],

time: 58.2 us -> 55.4 us (0.952)
  Pallas kernels: 54.6 us -> 51.8 us
    pallas_call x1, Pallas kernels: 52.4 us -> 49.6 us  [local(): pl.pallas_call(functools.partial(kernel, n, experts, count), out_shape=(j...]
where the time goes in v5:
time: 55.4 us; the launch traced here: 55.2 us
  Pallas kernels  51.8 us (94%)
  between operations  2.41 us (4%)
  local copies, waits for them, and re-layouts  1.03 us (2%)
    pallas_call x1, Pallas kernels, local(): pl.pallas_call(functools.partial(kernel, n, experts, count), out_shape=(j...  49.6 us
    pallas_call x1, Pallas kernels, hand_out(): pl.pallas_call(hand_out_kernel, out_shape=tuple((jax.ShapeDtypeStruct(a.s...  2.2 us

profile of v5, /device:TPU:0, one launch (start us, length us, event | category | flops | bytes accessed | tf_op | source)
XLA Modules:
  0.0 55.2 jit_solution(7255439767963399551)
XLA Ops:
  0.6 0.0 copy-start
  0.6 1.0 %copy-done = bf16[1,32,8192]{2,1,0:T(8,128)(2,1)S(1)} copy-done((bf16[1,32,8192]{2,1,0:T(8,128)(2,1)S(1)}, bf16[1,32,8192]{2,1,0:T(8,128)(2,1)}, u32[]{:S(2)}) %copy-start) | copy-done | bytes 524312
  1.7 49.6 %shard_map.66 = (f32[32,256]{1,0:T(8,128)S(1)}, f32[32,1024]{1,0:T(8,128)S(1)}, bf16[256,8192]{1,0:T(8,128)(2,1)S(1)}, f32[1,1]{1,0:T(1,128)}) custom-call(bf16[256,8192]{1,0:T(8,128)(2,1)} %bitcast.10, bf16[256,8192]{1,0:T(8,128)(2,1)} %bitcast.11, bf16[32,8192]{1,0:T(8,128)(2,1)S(1)} %bitcast.9), custom_call_target="tpu_custom_call" | custom-call | flops 671088640 | bytes 12582912 | tf_op jit(solution)/shard_map/pallas_call | solution.py:316
  51.2 2.2 %shard_map.67 = (f32[32,256]{1,0:T(8,128)}, f32[32,1024]{1,0:T(8,128)}, bf16[256,8192]{1,0:T(8,128)(2,1)}) custom-call(f32[32,256]{1,0:T(8,128)S(1)} %get-tuple-element.11.basis, f32[32,1024]{1,0:T(8,128)S(1)} %get-tuple-element.12.q, bf16[256,8192]{1,0:T(8,128)(2,1)S(1)} %get-tuple-element.13.new_error), custom_call_target="tpu_custom_call" | custom-call | tf_op jit(solution)/shard_map/pallas_call | solution.py:296
Async XLA Ops:
  0.6 1.0 %copy-start = (bf16[1,32,8192]{2,1,0:T(8,128)(2,1)S(1)}, bf16[1,32,8192]{2,1,0:T(8,128)(2,1)}, u32[]{:S(2)}) copy-start(bf16[1,32,8192]{2,1,0:T(8,128)(2,1)} %param.5) | copy-start | bytes 1572868

commit v6 on v5

--- a/solution.py
+++ b/solution.py
@@ -30,14 +30,13 @@
 
 def orthonormal_rows(pt):
     rank, rows = pt.shape
-    groups, halves = rank // GROUP, rows // LANES
+    groups = rank // GROUP
     padded = jnp.concatenate([pt, jnp.zeros((LANES - rank, rows), F32)], axis=0)
     gram = lax.dot_general(pt, padded, NT, precision=lax.Precision.HIGHEST, preferred_element_type=F32)
-    g = [gram[GROUP * i : GROUP * (i + 1), :] for i in range(groups)]
-    x = [
-        [pt[GROUP * i : GROUP * (i + 1), LANES * h : LANES * (h + 1)] for h in range(halves)]
-        for i in range(groups)
-    ]
+    lane = lax.broadcasted_iota(jnp.int32, (rank, LANES), 1)
+    line = lax.broadcasted_iota(jnp.int32, (rank, LANES), 0)
+    both = jnp.where(lane == line + rank, 1.0, gram)
+    g = [both[GROUP * i : GROUP * (i + 1), :] for i in range(groups)]
     row_id = lax.broadcasted_iota(jnp.int32, (GROUP, LANES), 0)
     for b in range(groups):
         below = range(b, groups)
@@ -56,18 +55,15 @@
                 row = spread_row(col[k][b], j)
                 for i in below:
                     col[k][i] = col[k][i] - factor[i] * row
-            for h in range(halves):
-                row = spread_row(x[b][h], j)
-                for i in below:
-                    x[i][h] = x[i][h] - factor[i] * row
-            if b + 1 < groups:
-                row = spread_row(g[b], j)
-                for i in below:
-                    g[i] = g[i] - factor[i] * row
-        scale = lax.rsqrt(pivots)
-        for h in range(halves):
-            x[b][h] = x[b][h] * scale
-    return jnp.concatenate([jnp.concatenate(parts, axis=1) for parts in x], axis=0)
+            row = spread_row(g[b], j)
+            for i in below:
+                g[i] = g[i] - factor[i] * row
+        g[b] = g[b] * lax.rsqrt(pivots)
+    solver = jnp.where(lane >= rank, jnp.concatenate(g, axis=0), 0.0)
+    padded = jnp.concatenate(
+        [jnp.zeros((rank, rows), F32), pt, jnp.zeros((LANES - 2 * rank, rows), F32)], axis=0
+    )
+    return jnp.dot(solver, padded, precision=lax.Precision.HIGHEST, preferred_element_type=F32)
 
 
 def kernel(

time: 55.4 us -> 55.7 us (level)
  no operation moved by 1% of the time
where the time goes in v6:
time: 55.7 us; the launch traced here: 55.5 us
  Pallas kernels  52.1 us (94%)
  between operations  2.41 us (4%)
  local copies, waits for them, and re-layouts  1.03 us (2%)
    pallas_call x1, Pallas kernels, local(): pl.pallas_call(functools.partial(kernel, n, experts, count), out_shape=(j...  49.9 us
    pallas_call x1, Pallas kernels, hand_out(): pl.pallas_call(hand_out_kernel, out_shape=tuple((jax.ShapeDtypeStruct(a.s...  2.2 us

profile of v6, /device:TPU:0, one launch (start us, length us, event | category | flops | bytes accessed | tf_op | source)
XLA Modules:
  0.0 55.5 jit_solution(2878850947809196692)
XLA Ops:
  0.6 0.0 copy-start
  0.6 1.0 %copy-done = bf16[1,32,8192]{2,1,0:T(8,128)(2,1)S(1)} copy-done((bf16[1,32,8192]{2,1,0:T(8,128)(2,1)S(1)}, bf16[1,32,8192]{2,1,0:T(8,128)(2,1)}, u32[]{:S(2)}) %copy-start) | copy-done | bytes 524312
  1.7 49.9 %shard_map.66 = (f32[32,256]{1,0:T(8,128)S(1)}, f32[32,1024]{1,0:T(8,128)S(1)}, bf16[256,8192]{1,0:T(8,128)(2,1)S(1)}, f32[1,1]{1,0:T(1,128)}) custom-call(bf16[256,8192]{1,0:T(8,128)(2,1)} %bitcast.10, bf16[256,8192]{1,0:T(8,128)(2,1)} %bitcast.11, bf16[32,8192]{1,0:T(8,128)(2,1)S(1)} %bitcast.9), custom_call_target="tpu_custom_call" | custom-call | flops 671088640 | bytes 12582912 | tf_op jit(solution)/shard_map/pallas_call | solution.py:312
  51.6 2.2 %shard_map.67 = (f32[32,256]{1,0:T(8,128)}, f32[32,1024]{1,0:T(8,128)}, bf16[256,8192]{1,0:T(8,128)(2,1)}) custom-call(f32[32,256]{1,0:T(8,128)S(1)} %get-tuple-element.11.basis, f32[32,1024]{1,0:T(8,128)S(1)} %get-tuple-element.12.q, bf16[256,8192]{1,0:T(8,128)(2,1)S(1)} %get-tuple-element.13.new_error), custom_call_target="tpu_custom_call" | custom-call | tf_op jit(solution)/shard_map/pallas_call | solution.py:292
Async XLA Ops:
  0.6 1.0 %copy-start = (bf16[1,32,8192]{2,1,0:T(8,128)(2,1)S(1)}, bf16[1,32,8192]{2,1,0:T(8,128)(2,1)}, u32[]{:S(2)}) copy-start(bf16[1,32,8192]{2,1,0:T(8,128)(2,1)} %param.5) | copy-start | bytes 1572868

commit v7 on v5

--- a/solution.py
+++ b/solution.py
@@ -13,6 +13,7 @@
 BF16 = jnp.bfloat16
 LANES = 128
 GROUP = 8
+HALF = 16
 NT = (((1,), (1,)), ((), ()))
 
 
@@ -67,7 +68,9 @@
         scale = lax.rsqrt(pivots)
         for h in range(halves):
             x[b][h] = x[b][h] * scale
-    return jnp.concatenate([jnp.concatenate(parts, axis=1) for parts in x], axis=0)
+        if (b + 1) * GROUP % HALF == 0:
+            done = x[b + 1 - HALF // GROUP : b + 1]
+            yield jnp.concatenate([jnp.concatenate(parts, axis=1) for parts in done], axis=0)
 
 
 def kernel(
@@ -75,7 +78,7 @@
     grad, error, q_init,
     basis, q_out, new_error, norm,
     g_buf, e_buf, comb, theirs, pair, fac0, fac,
-    s2_send, s2_recv, p, n1, n2,
+    s2_send, s2_recv, own, p, n1, n2,
     g_sem, e_sem, q_sem, o_sem,
     s1_ss, s1_rs, s2_ss, s2_rs, p_ss, p_rs,
     ag_ss, fw_ss, ag_rs, n1_ss, n1_rs, n2_ss, n2_rs,
@@ -162,45 +165,57 @@
         for j in range(1, n):
             pt = pt + p[it, j].astype(F32)
         pt = pt / n
-        ortho = orthonormal_rows(pt)
-        low = ortho.astype(BF16)
-
-        second_hop = []
-        for s in range(chips - 1, -1, -1):
-            q = jnp.dot(low, pair[xor(chip, s, chips)], preferred_element_type=F32)
-            if s:
-                s2_send[it, s] = q.astype(BF16)
-                second_hop.append(
-                    send(
-                        s2_send.at[it, s], s2_recv.at[it, s], s2_ss.at[it, s], s2_rs.at[it, s],
+        second_hop, ortho = [], []
+        for h, part in enumerate(orthonormal_rows(pt)):
+            ortho.append(part)
+            low = part.astype(BF16)
+            second_hop.append([])
+            for s in range(chips - 1, -1, -1):
+                q = jnp.dot(low, pair[xor(chip, s, chips)], preferred_element_type=F32)
+                if s:
+                    s2_send[it, h, s] = q.astype(BF16)
+                    copy = send(
+                        s2_send.at[it, h, s], s2_recv.at[it, h, s], s2_ss.at[it, h, s], s2_rs.at[it, h, s],
                         dp=2 * xor(chip, s, chips) + core,
                     )
-                )
-                second_hop[-1].start()
+                    copy.start()
+                    second_hop[h].append(copy)
+                else:
+                    own[h] = q
+
+        def half(j, h, it=it):
+            return fac.at[it, j, pl.ds(h * HALF, HALF), :]
+
+        halves = rank // HALF
+        for h in range(halves):
+            for copy in second_hop[h]:
+                copy.wait_recv()
+            q = own[h]
+            for s in range(1, chips):
+                q = q + s2_recv[it, h, s].astype(F32)
+            q = q / n
+            if last:
+                q_out[h * HALF : (h + 1) * HALF, :] = q
+            fac[it, me, h * HALF : (h + 1) * HALF, :] = q.astype(BF16)
+            for s in range(chips - 1, -1 if last else 0, -1):
+                target = partner if s == 0 else 2 * xor(chip, s, chips) + core
+                copy = send(half(me, h), half(me, h), ag_ss.at[it, h, s], ag_rs.at[it, h, me], dp=target)
+                copy.start()
+                pending.append(copy)
+            pending += second_hop[h]
         if last:
+            ortho = jnp.concatenate(ortho, axis=0)
             basis[...] = ortho
             low_t = jnp.transpose(ortho).astype(BF16)
-        for copy in second_hop:
-            copy.wait_recv()
-        for s in range(1, chips):
-            q = q + s2_recv[it, s].astype(F32)
-        q = q / n
-        pending += second_hop
-        if last:
-            q_out[...] = q
-        fac[it, me] = q.astype(BF16)
-
-        for s in range(chips - 1, -1 if last else 0, -1):
-            target = partner if s == 0 else 2 * xor(chip, s, chips) + core
-            copy = send(fac.at[it, me], fac.at[it, me], ag_ss.at[it, s], ag_rs.at[it, me], dp=target)
-            copy.start()
-            pending.append(copy)
-
-        def forward(s, j, it=it):
-            return send(fac.at[it, j], fac.at[it, j], fw_ss.at[s], ag_rs.at[it, j], dp=partner)
-
-        def arrived(j):
-            forward(0, j).wait_recv()
+
+        def forward(s, j, h, half=half, it=it):
+            return send(half(j, h), half(j, h), fw_ss.at[h, s], ag_rs.at[it, h, j], dp=partner)
+
+        def arrived(j, onward=None):
+            for h in range(halves):
+                forward(0, j, h).wait_recv()
+                if onward is not None:
+                    forward(onward, j, h).start()
 
         if not last:
             def use(t, value, it=it):
@@ -226,8 +241,7 @@
 
             def step(s, value):
                 t = xor(chip, s, chips)
-                arrived(2 * t + core)
-                forward(s, 2 * t + core).start()
+                arrived(2 * t + core, s)
                 value = use(2 * t + core, value)
                 arrived(2 * t + 1 - core)
                 return use(2 * t + 1 - core, value)
@@ -268,7 +282,8 @@
     for copy in pending:
         copy.wait_send()
     for s in range(1, chips):
-        forward(s, 2 * xor(chip, s, chips) + core).wait_send()
+        for h in range(halves):
+            forward(s, 2 * xor(chip, s, chips) + core, h).wait_send()
     for t in range(chips):
         hand_over(t).wait_send()
     for j in range(n):
@@ -312,7 +327,8 @@
     count = rows * width * n * experts
     dma = pltpu.SemaphoreType.DMA
     vmem, hbm = pl.BlockSpec(memory_space=pltpu.VMEM), pl.BlockSpec(memory_space=pl.ANY)
-    hop = pltpu.VMEM((ITERS, chips, rank, share), BF16)
+    halves = rank // HALF
+    hop = pltpu.VMEM((ITERS, halves, chips, HALF, share), BF16)
     basis, q, new_error, norm = pl.pallas_call(
         functools.partial(kernel, n, experts, count),
         out_shape=(
@@ -332,13 +348,14 @@
             pltpu.VMEM((n, rank, share), BF16),
             pltpu.VMEM((ITERS, n, rank, share), BF16),
             hop, hop,
+            pltpu.VMEM((halves, HALF, share), F32),
             pltpu.VMEM((ITERS, n, rank, rows), BF16),
             pltpu.VMEM((n, GROUP, LANES), F32),
             pltpu.VMEM((experts, GROUP, LANES), F32),
             dma((n,)), dma((n,)), dma((n,)), dma((n,)),
-            dma((chips,)), dma((chips,)), dma((ITERS, chips)), dma((ITERS, chips)),
+            dma((chips,)), dma((chips,)), dma((ITERS, halves, chips)), dma((ITERS, halves, chips)),
             dma((ITERS, n)), dma((ITERS, n)),
-            dma((ITERS, chips)), dma((chips,)), dma((ITERS, n)),
+            dma((ITERS, halves, chips)), dma((halves, chips)), dma((ITERS, halves, n)),
             dma((n,)), dma((n,)), dma((experts,)), dma((experts,)),
         ],
         compiler_params=pltpu.CompilerParams(

time: 55.4 us -> 53 us (0.957)
  Pallas kernels: 51.8 us -> 49.4 us
    pallas_call x1, Pallas kernels: 49.6 us -> 47.2 us  [local(): pl.pallas_call(functools.partial(kernel, n, experts, count), out_shape=(j...]
where the time goes in v7:
time: 53 us; the launch traced here: 52.8 us
  Pallas kernels  49.4 us (93%)
  between operations  2.41 us (5%)
  local copies, waits for them, and re-layouts  1.03 us (2%)
    pallas_call x1, Pallas kernels, local(): pl.pallas_call(functools.partial(kernel, n, experts, count), out_shape=(j...  47.2 us
    pallas_call x1, Pallas kernels, hand_out(): pl.pallas_call(hand_out_kernel, out_shape=tuple((jax.ShapeDtypeStruct(a.s...  2.2 us

profile of v7, /device:TPU:0, one launch (start us, length us, event | category | flops | bytes accessed | tf_op | source)
XLA Modules:
  0.0 52.8 jit_solution(11822388798572296134)
XLA Ops:
  0.6 0.0 copy-start
  0.6 1.0 %copy-done = bf16[1,32,8192]{2,1,0:T(8,128)(2,1)S(1)} copy-done((bf16[1,32,8192]{2,1,0:T(8,128)(2,1)S(1)}, bf16[1,32,8192]{2,1,0:T(8,128)(2,1)}, u32[]{:S(2)}) %copy-start) | copy-done | bytes 524312
  1.7 47.2 %shard_map.66 = (f32[32,256]{1,0:T(8,128)S(1)}, f32[32,1024]{1,0:T(8,128)S(1)}, bf16[256,8192]{1,0:T(8,128)(2,1)S(1)}, f32[1,1]{1,0:T(1,128)}) custom-call(bf16[256,8192]{1,0:T(8,128)(2,1)} %bitcast.10, bf16[256,8192]{1,0:T(8,128)(2,1)} %bitcast.11, bf16[32,8192]{1,0:T(8,128)(2,1)S(1)} %bitcast.9), custom_call_target="tpu_custom_call" | custom-call | flops 671088640 | bytes 12582912 | tf_op jit(solution)/shard_map/pallas_call | solution.py:332
  48.8 2.2 %shard_map.67 = (f32[32,256]{1,0:T(8,128)}, f32[32,1024]{1,0:T(8,128)}, bf16[256,8192]{1,0:T(8,128)(2,1)}) custom-call(f32[32,256]{1,0:T(8,128)S(1)} %get-tuple-element.11.basis, f32[32,1024]{1,0:T(8,128)S(1)} %get-tuple-element.12.q, bf16[256,8192]{1,0:T(8,128)(2,1)S(1)} %get-tuple-element.13.new_error), custom_call_target="tpu_custom_call" | custom-call | tf_op jit(solution)/shard_map/pallas_call | solution.py:311
Async XLA Ops:
  0.6 1.0 %copy-start = (bf16[1,32,8192]{2,1,0:T(8,128)(2,1)S(1)}, bf16[1,32,8192]{2,1,0:T(8,128)(2,1)}, u32[]{:S(2)}) copy-start(bf16[1,32,8192]{2,1,0:T(8,128)(2,1)} %param.5) | copy-start | bytes 1572868

commit v8 on v7

--- a/solution.py
+++ b/solution.py
@@ -27,6 +27,13 @@
 
 def spread_row(tile, j):
     return jnp.broadcast_to(tile[j : j + 1, :], tile.shape)
+
+
+def inverted(x):
+    guess = pl.reciprocal(x, approx=True)
+    for _ in range(2):
+        guess = guess * (2.0 - x * guess)
+    return guess
 
 
 def orthonormal_rows(pt):
@@ -50,9 +57,9 @@
         for j in range(GROUP):
             pivot = spread_row(col[j][b], j)
             pivots = jnp.where(row_id == j, pivot, pivots)
-            inverse = 1.0 / pivot
+            inverse = inverted(pivot)
+            col[j][b] = jnp.where(row_id > j, col[j][b], 0.0)
             factor = {i: col[j][i] * inverse for i in below}
-            factor[b] = jnp.where(row_id > j, factor[b], 0.0)
             for k in range(j + 1, GROUP):
                 row = spread_row(col[k][b], j)
                 for i in below:

time: 53 us -> 53.1 us (level)
  no operation moved by 1% of the time
where the time goes in v8:
time: 53.1 us; the launch traced here: 53 us
  Pallas kernels  49.5 us (93%)
  between operations  2.41 us (5%)
  local copies, waits for them, and re-layouts  1.03 us (2%)
    pallas_call x1, Pallas kernels, local(): pl.pallas_call(functools.partial(kernel, n, experts, count), out_shape=(j...  47.3 us
    pallas_call x1, Pallas kernels, hand_out(): pl.pallas_call(hand_out_kernel, out_shape=tuple((jax.ShapeDtypeStruct(a.s...  2.2 us

profile of v8, /device:TPU:0, one launch (start us, length us, event | category | flops | bytes accessed | tf_op | source)
XLA Modules:
  0.0 53.0 jit_solution(11636114298361317266)
XLA Ops:
  0.6 0.0 copy-start
  0.6 1.0 %copy-done = bf16[1,32,8192]{2,1,0:T(8,128)(2,1)S(1)} copy-done((bf16[1,32,8192]{2,1,0:T(8,128)(2,1)S(1)}, bf16[1,32,8192]{2,1,0:T(8,128)(2,1)}, u32[]{:S(2)}) %copy-start) | copy-done | bytes 524312
  1.7 47.3 %shard_map.66 = (f32[32,256]{1,0:T(8,128)S(1)}, f32[32,1024]{1,0:T(8,128)S(1)}, bf16[256,8192]{1,0:T(8,128)(2,1)S(1)}, f32[1,1]{1,0:T(1,128)}) custom-call(bf16[256,8192]{1,0:T(8,128)(2,1)} %bitcast.10, bf16[256,8192]{1,0:T(8,128)(2,1)} %bitcast.11, bf16[32,8192]{1,0:T(8,128)(2,1)S(1)} %bitcast.9), custom_call_target="tpu_custom_call" | custom-call | flops 671088640 | bytes 12582912 | tf_op jit(solution)/shard_map/pallas_call | solution.py:339
  49.0 2.2 %shard_map.67 = (f32[32,256]{1,0:T(8,128)}, f32[32,1024]{1,0:T(8,128)}, bf16[256,8192]{1,0:T(8,128)(2,1)}) custom-call(f32[32,256]{1,0:T(8,128)S(1)} %get-tuple-element.11.basis, f32[32,1024]{1,0:T(8,128)S(1)} %get-tuple-element.12.q, bf16[256,8192]{1,0:T(8,128)(2,1)S(1)} %get-tuple-element.13.new_error), custom_call_target="tpu_custom_call" | custom-call | tf_op jit(solution)/shard_map/pallas_call | solution.py:318
Async XLA Ops:
  0.6 1.0 %copy-start = (bf16[1,32,8192]{2,1,0:T(8,128)(2,1)S(1)}, bf16[1,32,8192]{2,1,0:T(8,128)(2,1)}, u32[]{:S(2)}) copy-start(bf16[1,32,8192]{2,1,0:T(8,128)(2,1)} %param.5) | copy-start | bytes 1572868
